TPU v7x, 512 devices: a whole 4x4x16 slice. The times are simulated.
512 devices in a mesh: sub: 32 (over z, core), blk: 16 (over y, x).
Axes of the slice: x: 4, y: 4, z: 16, core: 2. Of those that a mesh axis runs over, the one named last changes fastest.
Arguments:
- impedance: bfloat16 [32, 16384, 1024], P('sub', 'blk'), may hold values from -0.1875 to 0.1875
- port_node: int32 [32, 1024], P('sub', 'blk'), may hold values from 0 to 16383, as said below
- far_system: int32 [32, 1024], P('sub', 'blk'), may hold values from 0 to 31, as said below
- delays: int32 [32, 1024], P('sub', 'blk'), may hold values from 2 to 4, as said below
- admittance: float32 [32, 1024], P('sub', 'blk'), may hold values from 0.5 to 2
- pole_rates: float32 [32, 12, 1024], P('sub', None, 'blk'), may hold values from 0.05 to 0.95
- residues: float32 [32, 12, 1024], P('sub', None, 'blk'), may hold values from -1.8 to 1.8
- states: float32 [32, 12, 1024, 256], P('sub', None, 'blk'), may hold values from -3 to 3
- history: float32 [32, 4, 1024, 256], P('sub', None, 'blk'), may hold values from -6 to 6
- event_port: int32 [32, 256], P('sub'), may hold values from 0 to 1023
- amplitude: float32 [32, 2, 256], P('sub'), may hold values from -48 to 48
Outputs:
- peak_voltage: bfloat16 [32, 16384, 256], P('sub', 'blk')
- new_states: float32 [32, 12, 1024, 256], P('sub', None, 'blk')
- arrived: float32 [32, 1024, 2, 256], P('sub', 'blk')
Inputs may be any that keep to these rules, and one draw needn't show every extreme that they name: `port_node`: the node of terminal j lies in rows (j // 64) * 1024 to (j // 64 + 1) * 1024 - 1; the terminals of one subsystem have distinct nodes. Line j joins terminal j of two different subsystems: far_system[far_system[s, j], j] = s and far_system[s, j] != s. Of the terminals b * 64 to (b + 1) * 64 - 1 of one subsystem at most 6 lead to one same subsystem, and in every such group exactly 6 do for one of them. delays[s, j] = delays[far_system[s, j], j].
All inputs are finite; a program needn't handle non-finite values.
Results may differ from a plain program's by a relative error of at most 0.0042.
Values may be sent and summed in bfloat16 or wider, within the bound.
A program may use at most 64 MiB of HBM per device.

v0:
```python
import jax
import jax.numpy as jnp
from jax import lax
from jax.sharding import PartitionSpec as P


def pick_incident(history, delays, step_index):
    depth_iota = jnp.arange(history.shape[0], dtype=jnp.int32)
    wanted = delays - step_index - 1
    chosen = jnp.where(wanted[None, :, None] == depth_iota[:, None, None], history, 0.0)
    return jnp.sum(chosen, axis=0)


def deliver(emitted, partners):
    port_count = partners.shape[0]
    columns = emitted.shape[1]
    local_index = jnp.arange(port_count, dtype=jnp.int32)
    earlier = local_index[:, None] > local_index[None, :]
    slot_ranks = jnp.sum(jnp.logical_and(partners[:, None] == partners[None, :], earlier), axis=1)
    systems = lax.axis_size("sub")
    surplus = max(1, port_count // 16)
    capacity = (port_count - surplus + systems - 2) // (systems - 1) + surplus
    slot_rows = partners * capacity + slot_ranks
    outbox = jnp.zeros((systems * capacity, columns), jnp.float32).at[slot_rows].set(emitted)
    received = lax.all_to_all(
        outbox.reshape(systems, capacity, columns), "sub", split_axis=0, concat_axis=0, tiled=True
    )
    return received.reshape(systems * capacity, columns)[slot_rows]


def body(
    impedance,
    port_node,
    far_system,
    delays,
    admittance,
    pole_rates,
    residues,
    states,
    history,
    event_port,
    amplitude,
):
    node_rows = impedance.shape[1]
    port_count = port_node.shape[1]
    scenarios = states.shape[3]
    steps_total = amplitude.shape[1]
    block_index = lax.axis_index("blk")
    port_index = block_index * port_count + jnp.arange(port_count, dtype=jnp.int32)
    local_nodes = port_node[0] - block_index * node_rows
    matrix = impedance[0]
    decay_rates = pole_rates[0][:, :, None]
    weights = residues[0][:, :, None]
    partners = far_system[0]
    line_admittance = admittance[0][:, None]
    current = states[0]
    sources = []
    injections = []
    for step_index in range(steps_total):
        incident = pick_incident(history[0], delays[0], step_index)
        current = decay_rates * current + weights * incident[None]
        source = jnp.sum(current, axis=0)
        switched = jnp.where(
            event_port[0][None, :] == port_index[:, None], amplitude[0, step_index][None, :], 0.0
        )
        sources.append(source)
        injections.append((source + switched).astype(jnp.bfloat16))
    voltages = []
    arrivals = []
    for step_index in range(steps_total):
        voltage = jnp.dot(
            matrix,
            lax.all_gather(injections[step_index], "blk", axis=0, tiled=True),
            preferred_element_type=jnp.float32,
        )
        voltages.append(voltage)
        emitted_now = 2.0 * line_admittance * voltage[local_nodes] - sources[step_index]
        arrivals.append(deliver(emitted_now, partners))
    arrived = jnp.stack(arrivals, axis=1)
    peak_value = jnp.zeros((node_rows, scenarios), jnp.float32)
    for voltage in voltages:
        peak_value = jnp.maximum(peak_value, jnp.abs(voltage))
    return (peak_value.astype(jnp.bfloat16)[None], current[None], arrived[None])


def solution(mesh):
    placed = (
        P("sub", "blk", None),
        P("sub", "blk"),
        P("sub", "blk"),
        P("sub", "blk"),
        P("sub", "blk"),
        P("sub", None, "blk"),
        P("sub", None, "blk"),
        P("sub", None, "blk", None),
        P("sub", None, "blk", None),
        P("sub", None),
        P("sub", None, None),
    )
    return jax.shard_map(
        body,
        mesh=mesh,
        in_specs=placed,
        out_specs=(P("sub", "blk", None), P("sub", None, "blk", None), P("sub", "blk", None, None)),
        check_vma=False,
    )
```

profile of v0, /device:TPU:1, one launch (start us, length us, event | category | flops | bytes accessed | tf_op | source)
XLA Modules:
  0.0 123.7 jit_solution(7459575699059238528)
XLA Ops:
  0.6 0.8 add_bitcast_fusion
  1.5 0.8 fusion.34
  2.2 0.7 copy_bitcast_fusion
  2.9 1.1 fusion.13
  4.1 1.4 %fusion.11 = (f32[64,256]{1,0:T(8,128)S(1)}, f32[64,256]{1,0:T(8,128)S(1)}) fusion(f32[1,12,64,256]{3,2,1,0:T(8,128)} %param.18, f32[64,256]{1,0:T(8,128)S(1)} %get-tuple-element.14, f32[12,64]{1,0:T(8,128)S(1)} %get-tuple-element.24, f32[12,64]{1,0:T(8,128)S(1)} %get-tuple-element.25, f32[64,256]{1,0:T(8,128)S(1)} %get-tuple-element.15), kind=kLoop, calls=%fused_computation.17 | loop fusion | flops 1540096 | bytes 1054720 | tf_op jit(solution)/shard_map/reduce_sum | solution.py:62
  5.5 1.4 %fusion.20 = (bf16[64,256]{1,0:T(8,128)(2,1)S(1)}, bf16[64,256]{1,0:T(8,128)(2,1)}) fusion(f32[64,256]{1,0:T(8,128)S(1)} %get-tuple-element.12, f32[256]{0:T(256)S(1)} %bitcast.64, s32[256]{0:T(256)} %bitcast.66, s32[64]{0:T(128)S(1)} %iota_add_fusion, f32[64,256]{1,0:T(8,128)S(1)} %get-tuple-element.13, f32[256]{0:T(256)S(1)} %bitcast.65), kind=kLoop, calls=%fused_computation.31 | loop fusion | flops 114688 | bytes 199936 | tf_op jit(solution)/shard_map/convert_element_type | solution.py:67
  6.9 20.0 %all_gather.6 = bf16[1024,256]{1,0:T(8,128)(2,1)S(1)} all-gather(bf16[64,256]{1,0:T(8,128)(2,1)S(1)} %get-tuple-element.18), channel_id=1, replica_groups=mesh['sub'=32,'blk'=16] {'blk'}, dimensions={0}, use_global_device_ids=true | all-gather | bytes 557056 | tf_op jit(solution)/shard_map/all_gather | solution.py:73
  26.9 0.8 fusion.4
  27.7 1.3 %copy.22 = f32[1024,256]{1,0:T(8,128)} copy(f32[1024,256]{0,1:T(8,128)S(1)} %fusion.4) | data formatting | bytes 2097152 | tf_op jit(solution)/shard_map/dot_general | solution.py:71
  30.9 2.2 %scatter_custom_fusion = f32[192,256]{1,0:T(8,128)S(1)} fusion(s32[64]{0:T(128)} %fusion.30, f32[]{:T(128)} %constant.11.clone.1, f32[64,256]{1,0:T(8,128)S(1)} %get-tuple-element.12, f32[64]{0:T(128)} %multiply_bitcast_fusion, f32[1024,256]{1,0:T(8,128)} %copy.22, s32[1024]{0:T(1024)} %pad_clamp_fusion.1), kind=kCustom, calls=%fused_computation.26 | custom fusion | flops 32768 | bytes 1315840 | tf_op jit(solution)/shard_map/scatter | solution.py:24
  33.0 0.7 reshape.153
  33.8 21.0 %all-to-all-start = ((f32[32,6,256]{2,1,0:T(8,128)}), f32[32,6,256]{2,1,0:T(8,128)S(1)}, u32[]{:S(2)}, u32[]{:S(2)}) async-start(f32[32,6,256]{2,1,0:T(8,128)} %reshape.153), calls=%async_computation | async-start | bytes 524288 | tf_op jit(solution)/shard_map/all_to_all | solution.py:25
  54.8 19.7 %all_gather.7 = bf16[1024,256]{1,0:T(8,128)(2,1)S(1)} all-gather(bf16[64,256]{1,0:T(8,128)(2,1)} %get-tuple-element.19), channel_id=1, replica_groups=mesh['sub'=32,'blk'=16] {'blk'}, dimensions={0}, use_global_device_ids=true | all-gather | bytes 557056 | tf_op jit(solution)/shard_map/all_gather | solution.py:73
  74.5 1.8 %fusion.7 = f32[1024,256]{0,1:T(8,128)} fusion(bf16[1024,256]{1,0:T(8,128)(2,1)S(1)} %all_gather.7, bf16[1,1024,1024]{2,1,0:T(8,128)(2,1)S(1)} %copy-done), kind=kOutput, calls=%fused_computation.11 | convolution fusion | flops 536870912 | bytes 3670016 | tf_op jit(solution)/shard_map/dot_general | solution.py:71
  76.3 2.6 %copy.23 = f32[1024,256]{1,0:T(8,128)} copy(f32[1024,256]{0,1:T(8,128)} %fusion.7) | data formatting | bytes 2097152 | tf_op jit(solution)/shard_map/dot_general | solution.py:71
  78.9 2.8 %scatter_custom_fusion.1 = f32[192,256]{1,0:T(8,128)} fusion(s32[64]{0:T(128)} %fusion.30, f32[]{:T(128)} %constant.11.clone.1, f32[64,256]{1,0:T(8,128)S(1)} %get-tuple-element.13, f32[64]{0:T(128)} %multiply_bitcast_fusion, f32[1024,256]{1,0:T(8,128)} %copy.23, s32[1024]{0:T(1024)} %pad_clamp_fusion.1), kind=kCustom, calls=%fused_computation.24 | custom fusion | flops 32768 | bytes 1315840 | tf_op jit(solution)/shard_map/scatter | solution.py:24
  81.6 1.7 %reshape.155 = f32[32,6,256]{2,1,0:T(8,128)} reshape(f32[192,256]{1,0:T(8,128)} %scatter_custom_fusion.1) | data formatting | bytes 393216 | tf_op jit(solution)/shard_map/reshape | solution.py:26
  83.3 16.0 %all-to-all-start.1 = ((f32[32,6,256]{2,1,0:T(8,128)}), f32[32,6,256]{2,1,0:T(8,128)}, u32[]{:S(2)}, u32[]{:S(2)}) async-start(f32[32,6,256]{2,1,0:T(8,128)} %reshape.155), calls=%async_computation.1 | async-start | bytes 524288 | tf_op jit(solution)/shard_map/all_to_all | solution.py:25
  99.3 2.2 %fusion.12 = bf16[1,1024,256]{1,2,0:T(8,128)(2,1)} fusion(f32[1024,256]{0,1:T(8,128)} %fusion.7, f32[1024,256]{0,1:T(8,128)S(1)} %fusion.4), kind=kLoop, calls=%fused_computation.18 | loop fusion | flops 1310720 | bytes 2621440 | tf_op jit(solution)/shard_map/broadcast_in_dim | solution.py:83
  101.5 2.0 %copy.24 = bf16[1,1024,256]{2,1,0:T(8,128)(2,1)} copy(bf16[1,1024,256]{1,2,0:T(8,128)(2,1)} %fusion.12) | data formatting | bytes 1048576
  104.2 2.3 %multiply_add_fusion = f32[1,12,64,256]{3,2,1,0:T(8,128)} fusion(f32[1,12,64,256]{3,2,1,0:T(8,128)} %param.18, f32[64,256]{1,0:T(8,128)S(1)} %copy-done.2, f32[64,256]{1,0:T(8,128)S(1)} %get-tuple-element.14, f32[12,64]{1,0:T(8,128)S(1)} %get-tuple-element.24, f32[12,64]{1,0:T(8,128)S(1)} %get-tuple-element.25), kind=kLoop, calls=%fused_computation.15 | loop fusion | flops 1179648 | bytes 1710080 | tf_op jit(solution)/shard_map/add | solution.py:61
  107.2 14.1 %all-to-all-done.1 = f32[32,6,256]{2,1,0:T(8,128)} async-done(((f32[32,6,256]{2,1,0:T(8,128)}), f32[32,6,256]{2,1,0:T(8,128)}, u32[]{:S(2)}, u32[]{:S(2)}) %all-to-all-start.1) | async-done | bytes 196640 | tf_op jit(solution)/shard_map/all_to_all | solution.py:25
  121.3 1.0 reshape.156
  123.0 0.8 copy.25
  (25 shorter events, 3.9 us)
Async XLA Ops:
  0.6 26.2 %copy-start = (bf16[1,1024,1024]{2,1,0:T(8,128)(2,1)S(1)}, bf16[1,1024,1024]{2,1,0:T(8,128)(2,1)}, u32[]{:S(2)}) copy-start(bf16[1,1024,1024]{2,1,0:T(8,128)(2,1)} %param.11) | copy-start | bytes 6291460
  4.0 2.8 %copy-start.1 = (f32[64,256]{1,0:T(8,128)}, f32[64,256]{1,0:T(8,128)S(1)}, u32[]{:S(2)}) copy-start(f32[64,256]{1,0:T(8,128)S(1)} %get-tuple-element.15) | copy-start | bytes 196612
  26.9 2.1 %copy-start.3 = (s32[1,64]{1,0:T(1,128)S(1)}, s32[1,64]{1,0:T(1,128)}, u32[]{:S(2)}) copy-start(s32[1,64]{1,0:T(1,128)} %param.12) | copy-start | bytes 772
  26.9 2.7 %copy-start.4 = (s32[1,64]{1,0:T(1,128)S(1)}, s32[1,64]{1,0:T(1,128)}, u32[]{:S(2)}) copy-start(s32[1,64]{1,0:T(1,128)} %param.13) | copy-start | bytes 772
  26.9 3.5 %copy-start.5 = (f32[1,64]{1,0:T(1,128)S(1)}, f32[1,64]{1,0:T(1,128)}, u32[]{:S(2)}) copy-start(f32[1,64]{1,0:T(1,128)} %param.15) | copy-start | bytes 772
  33.8 49.5 %all-to-all-start = ((f32[32,6,256]{2,1,0:T(8,128)}), f32[32,6,256]{2,1,0:T(8,128)S(1)}, u32[]{:S(2)}, u32[]{:S(2)}) async-start(f32[32,6,256]{2,1,0:T(8,128)} %reshape.153), calls=%async_computation | async-start | bytes 524288 | tf_op jit(solution)/shard_map/all_to_all | solution.py:25
  83.3 20.9 %copy-start.2 = (f32[64,256]{1,0:T(8,128)S(1)}, f32[64,256]{1,0:T(8,128)}, u32[]{:S(2)}) copy-start(f32[64,256]{1,0:T(8,128)} %copy-done.1) | copy-start | bytes 196612
  83.3 38.0 %all-to-all-start.1 = ((f32[32,6,256]{2,1,0:T(8,128)}), f32[32,6,256]{2,1,0:T(8,128)}, u32[]{:S(2)}, u32[]{:S(2)}) async-start(f32[32,6,256]{2,1,0:T(8,128)} %reshape.155), calls=%async_computation.1 | async-start | bytes 524288 | tf_op jit(solution)/shard_map/all_to_all | solution.py:25
where the time goes:
time: 125 us; the launch traced here: 124 us
  blocking collectives  39.7 us (32%)
  starting transfers between devices  37 us (30%)
  other arithmetic  16.7 us (13%)
  waiting for transfers between devices  14.1 us (11%)
  local copies, waits for them, and re-layouts  12.9 us (10%)
  matrix products  2.53 us (2%)
    all_gather x2, blocking collectives, body(): lax.all_gather(injections[step_index], 'blk', axis=0, tiled=True)  39.7 us
    all_to_all x2, starting transfers between devices, deliver(): lax.all_to_all(outbox.reshape(systems, capacity, columns), 'sub', split_a...  37 us
    all_to_all x2, waiting for transfers between devices, deliver(): lax.all_to_all(outbox.reshape(systems, capacity, columns), 'sub', split_a...  14.1 us
    scatter x2, other arithmetic, deliver(): jnp.zeros((systems * capacity, columns), jnp.float32).at[slot_rows]  4.9 us
    dot_general x2, local copies, waits for them, and re-layouts, body(): jnp.dot(matrix, lax.all_gather(injections[step_index], 'blk', axis=0, til...  3.92 us
    unnamed x15, local copies, waits for them, and re-layouts  3.55 us
    dot_general x2, matrix products, body(): jnp.dot(matrix, lax.all_gather(injections[step_index], 'blk', axis=0, til...  2.53 us
  transfers between devices with their start and end apart: 2, of which 1 were waited for; matrix products, arithmetic and copies ran while one was open for 13% of the time, Pallas kernels for 0%

commit v1 on v0

--- a/solution.py
+++ b/solution.py
@@ -70,7 +70,12 @@
     for step_index in range(steps_total):
         voltage = jnp.dot(
             matrix,
-            lax.all_gather(injections[step_index], "blk", axis=0, tiled=True),
+            jnp.concatenate(
+                lax.all_to_all(
+                    jnp.stack([injections[step_index]] * lax.axis_size("blk")), "blk", 0, 0
+                ),
+                axis=0,
+            ),
             preferred_element_type=jnp.float32,
         )
         voltages.append(voltage)

time: 125 us -> 111 us (0.89)
  blocking collectives: 39.7 us -> 0 us
  waiting for transfers between devices: 14.1 us -> 37.9 us
  local copies, waits for them, and re-layouts: 12.9 us -> 15.3 us
  matrix products: 2.53 us -> 4.56 us
  other arithmetic: 16.7 us -> 14.9 us
    all_gather x2 -> x0, blocking collectives: 39.7 us -> none  [body(): lax.all_gather(injections[step_index], 'blk', axis=0, tiled=True)]
    all_to_all x2, waiting for transfers between devices: 14.1 us -> 27.5 us  [deliver(): lax.all_to_all(outbox.reshape(systems, capacity, columns), 'sub', split_a...]
    all_to_all x0 -> x2, starting transfers between devices: none -> 11.8 us  [body(): lax.all_to_all(jnp.stack([injections[step_index]] * lax.axis_size('blk'))...]
    all_to_all x2, starting transfers between devices: 37 us -> 25.3 us  [deliver(): lax.all_to_all(outbox.reshape(systems, capacity, columns), 'sub', split_a...]
    all_to_all x0 -> x2, waiting for transfers between devices: none -> 10.3 us  [body(): lax.all_to_all(jnp.stack([injections[step_index]] * lax.axis_size('blk'))...]
    dot_general x2, matrix products: 2.53 us -> 4.56 us  [body(): jnp.dot(matrix, jnp.concatenate(lax.all_to_all(jnp.stack([injections[step...]
    another operation x0 -> x2, local copies, waits for them, and re-layouts: none -> 1.74 us  [body(): jnp.stack([injections[step_index]] * lax.axis_size('blk'))]
    unnamed x15 -> x17, local copies, waits for them, and re-layouts: 3.55 us -> 4.16 us
  transfers between devices with their start and end apart: 2 -> 4, of which waited for: 1 -> 4; matrix products, arithmetic and copies ran while one was open for 13% -> 22% of each run, Pallas kernels for 0% -> 0%
where the time goes in v1:
time: 111 us; the launch traced here: 110 us
  waiting for transfers between devices  37.9 us (34%)
  starting transfers between devices  37.1 us (33%)
  local copies, waits for them, and re-layouts  15.3 us (14%)
  other arithmetic  14.9 us (13%)
  matrix products  4.56 us (4%)
    all_to_all x2, waiting for transfers between devices, deliver(): lax.all_to_all(outbox.reshape(systems, capacity, columns), 'sub', split_a...  27.5 us
    all_to_all x2, starting transfers between devices, deliver(): lax.all_to_all(outbox.reshape(systems, capacity, columns), 'sub', split_a...  25.3 us
    all_to_all x2, starting transfers between devices, body(): lax.all_to_all(jnp.stack([injections[step_index]] * lax.axis_size('blk'))...  11.8 us
    all_to_all x2, waiting for transfers between devices, body(): lax.all_to_all(jnp.stack([injections[step_index]] * lax.axis_size('blk'))...  10.3 us
    scatter x2, other arithmetic, deliver(): jnp.zeros((systems * capacity, columns), jnp.float32).at[slot_rows]  4.92 us
    dot_general x2, matrix products, body(): jnp.dot(matrix, jnp.concatenate(lax.all_to_all(jnp.stack([injections[step...  4.56 us
    unnamed x17, local copies, waits for them, and re-layouts  4.16 us
    dot_general x2, local copies, waits for them, and re-layouts, body(): jnp.dot(matrix, jnp.concatenate(lax.all_to_all(jnp.stack([injections[step...  3.88 us
  transfers between devices with their start and end apart: 4, of which 4 were waited for; matrix products, arithmetic and copies ran while one was open for 22% of the time, Pallas kernels for 0%

profile of v1, /device:TPU:1, one launch (start us, length us, event | category | flops | bytes accessed | tf_op | source)
XLA Modules:
  0.0 110.4 jit_solution(17903432958933525136)
XLA Ops:
  0.7 0.8 add_bitcast_fusion
  3.0 1.1 fusion.13
  4.7 1.4 %fusion.11 = (f32[64,256]{1,0:T(8,128)S(1)}, f32[64,256]{1,0:T(8,128)S(1)}) fusion(f32[1,12,64,256]{3,2,1,0:T(8,128)} %param.18, f32[64,256]{1,0:T(8,128)S(1)} %get-tuple-element.14, f32[12,64]{1,0:T(8,128)S(1)} %get-tuple-element.24, f32[12,64]{1,0:T(8,128)S(1)} %get-tuple-element.25, f32[64,256]{1,0:T(8,128)S(1)} %get-tuple-element.15), kind=kLoop, calls=%fused_computation.17 | loop fusion | flops 1540096 | bytes 1054720 | tf_op jit(solution)/shard_map/reduce_sum | solution.py:62
  6.9 0.8 stack.10
  7.7 7.6 %all-to-all-start = ((bf16[16,64,256]{2,1,0:T(8,128)(2,1)}), bf16[16,64,256]{2,1,0:T(8,128)(2,1)S(1)}, u32[]{:S(2)}, u32[]{:S(2)}) async-start(bf16[16,64,256]{2,1,0:T(8,128)(2,1)} %stack.10), calls=%async_computation | async-start | bytes 1048576 | tf_op jit(solution)/shard_map/all_to_all | solution.py:74
  16.7 7.7 %all-to-all-done = bf16[16,64,256]{2,1,0:T(8,128)(2,1)S(1)} async-done(((bf16[16,64,256]{2,1,0:T(8,128)(2,1)}), bf16[16,64,256]{2,1,0:T(8,128)(2,1)S(1)}, u32[]{:S(2)}, u32[]{:S(2)}) %all-to-all-start) | async-done | bytes 524320 | tf_op jit(solution)/shard_map/all_to_all | solution.py:74
  24.3 0.9 stack.11
  25.2 4.2 %all-to-all-start.1 = ((bf16[16,64,256]{2,1,0:T(8,128)(2,1)}), bf16[16,64,256]{2,1,0:T(8,128)(2,1)}, u32[]{:S(2)}, u32[]{:S(2)}) async-start(bf16[16,64,256]{2,1,0:T(8,128)(2,1)} %stack.11), calls=%async_computation.1 | async-start | bytes 1048576 | tf_op jit(solution)/shard_map/all_to_all | solution.py:74
  30.0 1.8 %fusion.4 = f32[1024,256]{0,1:T(8,128)S(1)} fusion(bf16[1024,256]{1,0:T(8,128)(2,1)} %bitcast.64, bf16[1,1024,1024]{2,1,0:T(8,128)(2,1)S(1)} %copy-done), kind=kOutput, calls=%fused_computation.10 | convolution fusion | flops 536870912 | bytes 3670016 | tf_op jit(solution)/shard_map/dot_general | solution.py:71
  31.8 1.3 %copy.22 = f32[1024,256]{1,0:T(8,128)} copy(f32[1024,256]{0,1:T(8,128)S(1)} %fusion.4) | data formatting | bytes 2097152 | tf_op jit(solution)/shard_map/dot_general | solution.py:71
  33.1 2.2 %scatter_custom_fusion = f32[192,256]{1,0:T(8,128)S(1)} fusion(s32[64]{0:T(128)} %fusion.30, f32[]{:T(128)} %constant.11.clone.1, f32[64,256]{1,0:T(8,128)S(1)} %get-tuple-element.12, f32[64]{0:T(128)} %multiply_bitcast_fusion, f32[1024,256]{1,0:T(8,128)} %copy.22, s32[1024]{0:T(1024)} %pad_clamp_fusion.1), kind=kCustom, calls=%fused_computation.26 | custom fusion | flops 32768 | bytes 1315840 | tf_op jit(solution)/shard_map/scatter | solution.py:24
  36.0 2.7 %all-to-all-done.1 = bf16[16,64,256]{2,1,0:T(8,128)(2,1)} async-done(((bf16[16,64,256]{2,1,0:T(8,128)(2,1)}), bf16[16,64,256]{2,1,0:T(8,128)(2,1)}, u32[]{:S(2)}, u32[]{:S(2)}) %all-to-all-start.1) | async-done | bytes 524320 | tf_op jit(solution)/shard_map/all_to_all | solution.py:74
  38.7 20.1 %all-to-all-start.2 = ((f32[32,6,256]{2,1,0:T(8,128)}), f32[32,6,256]{2,1,0:T(8,128)S(1)}, u32[]{:S(2)}, u32[]{:S(2)}) async-start(f32[32,6,256]{2,1,0:T(8,128)} %reshape.219), calls=%async_computation.2 | async-start | bytes 524288 | tf_op jit(solution)/shard_map/all_to_all | solution.py:25
  58.8 2.8 %fusion.7 = f32[1024,256]{0,1:T(8,128)} fusion(bf16[1024,256]{1,0:T(8,128)(2,1)} %bitcast.10, bf16[1,1024,1024]{2,1,0:T(8,128)(2,1)S(1)} %copy-done), kind=kOutput, calls=%fused_computation.11 | convolution fusion | flops 536870912 | bytes 3670016 | tf_op jit(solution)/shard_map/dot_general | solution.py:71
  61.5 2.6 %copy.23 = f32[1024,256]{1,0:T(8,128)} copy(f32[1024,256]{0,1:T(8,128)} %fusion.7) | data formatting | bytes 2097152 | tf_op jit(solution)/shard_map/dot_general | solution.py:71
  64.1 2.8 %scatter_custom_fusion.1 = f32[192,256]{1,0:T(8,128)} fusion(s32[64]{0:T(128)} %fusion.30, f32[]{:T(128)} %constant.11.clone.1, f32[64,256]{1,0:T(8,128)S(1)} %get-tuple-element.13, f32[64]{0:T(128)} %multiply_bitcast_fusion, f32[1024,256]{1,0:T(8,128)} %copy.23, s32[1024]{0:T(1024)} %pad_clamp_fusion.1), kind=kCustom, calls=%fused_computation.24 | custom fusion | flops 32768 | bytes 1315840 | tf_op jit(solution)/shard_map/scatter | solution.py:24
  66.9 1.7 %reshape.221 = f32[32,6,256]{2,1,0:T(8,128)} reshape(f32[192,256]{1,0:T(8,128)} %scatter_custom_fusion.1) | data formatting | bytes 393216 | tf_op jit(solution)/shard_map/reshape | solution.py:26
  68.5 12.2 %all-to-all-done.2 = f32[32,6,256]{2,1,0:T(8,128)S(1)} async-done(((f32[32,6,256]{2,1,0:T(8,128)}), f32[32,6,256]{2,1,0:T(8,128)S(1)}, u32[]{:S(2)}, u32[]{:S(2)}) %all-to-all-start.2) | async-done | bytes 196640 | tf_op jit(solution)/shard_map/all_to_all | solution.py:25
  80.8 5.2 %all-to-all-start.3 = ((f32[32,6,256]{2,1,0:T(8,128)}), f32[32,6,256]{2,1,0:T(8,128)}, u32[]{:S(2)}, u32[]{:S(2)}) async-start(f32[32,6,256]{2,1,0:T(8,128)} %reshape.221), calls=%async_computation.3 | async-start | bytes 524288 | tf_op jit(solution)/shard_map/all_to_all | solution.py:25
  86.7 2.3 %multiply_add_fusion = f32[1,12,64,256]{3,2,1,0:T(8,128)} fusion(f32[1,12,64,256]{3,2,1,0:T(8,128)} %param.18, f32[64,256]{1,0:T(8,128)} %copy-done.3, f32[64,256]{1,0:T(8,128)S(1)} %get-tuple-element.14, f32[12,64]{1,0:T(8,128)S(1)} %get-tuple-element.24, f32[12,64]{1,0:T(8,128)S(1)} %get-tuple-element.25), kind=kLoop, calls=%fused_computation.15 | loop fusion | flops 1179648 | bytes 1710080 | tf_op jit(solution)/shard_map/add | solution.py:61
  89.0 1.0 fusion.12
  90.0 2.0 %copy.24 = bf16[1,1024,256]{2,1,0:T(8,128)(2,1)} copy(bf16[1,1024,256]{1,2,0:T(8,128)(2,1)} %fusion.12) | data formatting | bytes 1048576
  92.7 15.3 %all-to-all-done.3 = f32[32,6,256]{2,1,0:T(8,128)} async-done(((f32[32,6,256]{2,1,0:T(8,128)}), f32[32,6,256]{2,1,0:T(8,128)}, u32[]{:S(2)}, u32[]{:S(2)}) %all-to-all-start.3) | async-done | bytes 196640 | tf_op jit(solution)/shard_map/all_to_all | solution.py:25
  108.0 1.0 reshape.222
  (31 shorter events, 8.3 us)
Async XLA Ops:
  0.6 29.4 %copy-start = (bf16[1,1024,1024]{2,1,0:T(8,128)(2,1)S(1)}, bf16[1,1024,1024]{2,1,0:T(8,128)(2,1)}, u32[]{:S(2)}) copy-start(bf16[1,1024,1024]{2,1,0:T(8,128)(2,1)} %param.11) | copy-start | bytes 6291460
  0.6 14.7 %copy-start.4 = (s32[1,64]{1,0:T(1,128)S(1)}, s32[1,64]{1,0:T(1,128)}, u32[]{:S(2)}) copy-start(s32[1,64]{1,0:T(1,128)} %param.12) | copy-start | bytes 772
  0.7 15.3 %copy-start.5 = (s32[1,64]{1,0:T(1,128)S(1)}, s32[1,64]{1,0:T(1,128)}, u32[]{:S(2)}) copy-start(s32[1,64]{1,0:T(1,128)} %param.13) | copy-start | bytes 772
  4.1 0.6 copy-start.3
  4.7 24.8 %copy-start.6 = (f32[1,64]{1,0:T(1,128)S(1)}, f32[1,64]{1,0:T(1,128)}, u32[]{:S(2)}) copy-start(f32[1,64]{1,0:T(1,128)} %param.15) | copy-start | bytes 772
  7.7 16.6 %all-to-all-start = ((bf16[16,64,256]{2,1,0:T(8,128)(2,1)}), bf16[16,64,256]{2,1,0:T(8,128)(2,1)S(1)}, u32[]{:S(2)}, u32[]{:S(2)}) async-start(bf16[16,64,256]{2,1,0:T(8,128)(2,1)} %stack.10), calls=%async_computation | async-start | bytes 1048576 | tf_op jit(solution)/shard_map/all_to_all | solution.py:74
  24.3 5.7 %copy-start.2 = (bf16[16,64,256]{2,1,0:T(8,128)(2,1)}, bf16[16,64,256]{2,1,0:T(8,128)(2,1)S(1)}, u32[]{:S(2)}) copy-start(bf16[16,64,256]{2,1,0:T(8,128)(2,1)S(1)} %all-to-all-done) | copy-start | bytes 1572868
  25.2 13.5 %all-to-all-start.1 = ((bf16[16,64,256]{2,1,0:T(8,128)(2,1)}), bf16[16,64,256]{2,1,0:T(8,128)(2,1)}, u32[]{:S(2)}, u32[]{:S(2)}) async-start(bf16[16,64,256]{2,1,0:T(8,128)(2,1)} %stack.11), calls=%async_computation.1 | async-start | bytes 1048576 | tf_op jit(solution)/shard_map/all_to_all | solution.py:74
  38.7 42.1 %all-to-all-start.2 = ((f32[32,6,256]{2,1,0:T(8,128)}), f32[32,6,256]{2,1,0:T(8,128)S(1)}, u32[]{:S(2)}, u32[]{:S(2)}) async-start(f32[32,6,256]{2,1,0:T(8,128)} %reshape.219), calls=%async_computation.2 | async-start | bytes 524288 | tf_op jit(solution)/shard_map/all_to_all | solution.py:25
  80.8 27.2 %all-to-all-start.3 = ((f32[32,6,256]{2,1,0:T(8,128)}), f32[32,6,256]{2,1,0:T(8,128)}, u32[]{:S(2)}, u32[]{:S(2)}) async-start(f32[32,6,256]{2,1,0:T(8,128)} %reshape.221), calls=%async_computation.3 | async-start | bytes 524288 | tf_op jit(solution)/shard_map/all_to_all | solution.py:25
  86.0 3.0 %copy-start.1 = (f32[1024,256]{0,1:T(8,128)S(1)}, f32[1024,256]{0,1:T(8,128)}, u32[]{:S(2)}) copy-start(f32[1024,256]{0,1:T(8,128)} %fusion.7) | copy-start | bytes 3145732
